TPU v7x, 256 devices: a whole 4x4x8 slice. The times are simulated.
256 devices in a mesh: wide: 32 (over y, x, core), narrow: 8 (over z).
Axes of the slice: x: 4, y: 4, z: 8, core: 2. Of those that a mesh axis runs over, the one named last changes fastest.
Arguments:
- noise: float32 [1024, 1024, 128], P('narrow', 'wide'), may hold values from -6 to 6
- spectrum: float32 [128, 1024, 1024], P('wide', None, 'narrow'), may hold values from 0.1 to 8.5, as said below
- assay: bfloat16 [256, 512], P(('wide', 'narrow')), may hold values from -5 to 5
- measure_weights: bfloat16 [256, 512, 4, 128], P(('wide', 'narrow')), may hold values from -3 to 3
- measure_owner: int32 [256, 512], P(('wide', 'narrow')), may hold values from 0 to 255, as said below
- measure_cell: int32 [256, 512], P(('wide', 'narrow')), may hold values from 0 to 524287
- measure_pencils: int32 [256, 512, 4], P(('wide', 'narrow')), may hold values from 0 to 4095
Outputs:
- conditioned: float32 [1024, 1024, 128], P('narrow', 'wide')
Inputs may be any that keep to these rules, and one draw needn't show every extreme that they name: `spectrum`: Positive, with rough factors from frequency to frequency. `measure_owner`: devices are numbered with narrow fastest. At most 8 measurements of one device share an owner; one owner, drawn from the seed, receives exactly 8 from every device. `measure_cell`: cells of the owner's block are numbered with z fastest, then y, then x. `measure_pencils`: pencils of the owner's block are numbered with y fastest.
All inputs are finite; a program needn't handle non-finite values.
Results may differ from a plain program's by a relative error of at most 0.0003.
Values may be sent and summed in bfloat16 or wider, within the bound.
A program may use at most 128 MiB of HBM per device.

v0:
```python
import math
import jax
import jax.numpy as jnp
from jax import lax
from jax.sharding import PartitionSpec as P

CELLS_FIRST = 1024
CELLS_SECOND = 1024
CELLS_THIRD = 128
TARGET_PENCILS = 4
highest = lax.Precision.HIGHEST


def pair_tables(cosine, sine):
    upper = jnp.stack([cosine, sine], axis=1)
    lower = jnp.stack([-sine, cosine], axis=1)
    return jnp.stack([upper, lower])


def dft_matrix(length, sign):
    index = jnp.arange(length, dtype=jnp.int32)
    phase = index[:, None] * index[None, :] % length
    angle = phase.astype(jnp.float32) * (2.0 * math.pi / length)
    return pair_tables(jnp.cos(angle), sign * jnp.sin(angle))


def slot_depth(depth, half):
    slots = jnp.arange(depth, dtype=jnp.int32)
    span = 2 * half
    base = slots // span * half + slots % span % half
    mirror = jnp.where(base > 0, depth - base, depth // 2)
    return jnp.where(slots % span < half, base, mirror)


def arranged_tables(depth, half, sign):
    depth_of = slot_depth(depth, half)
    cell_list = jnp.arange(depth, dtype=jnp.int32)
    phase = depth_of[:, None] * cell_list[None, :] % depth
    angle = phase.astype(jnp.float32) * (2.0 * math.pi / depth)
    return (jnp.cos(angle), sign * jnp.sin(angle))


def transform(block, sign):
    outer = block.shape[1]
    length = block.shape[2]
    inner = block.shape[3]
    rows_q = 128
    rows_p = length // rows_q
    four = block.reshape(2, outer, rows_p, rows_q, inner)
    four = jnp.einsum("sapqb,sptc->tacqb", four, dft_matrix(rows_p, sign), precision=highest)
    index_p = jnp.arange(rows_p, dtype=jnp.int32)
    index_q = jnp.arange(rows_q, dtype=jnp.int32)
    angle = (index_p[:, None] * index_q[None, :] % length).astype(jnp.float32) * (
        2.0 * math.pi / length
    )
    twist_cos = jnp.cos(angle)[None, :, :, None]
    twist_sin = (sign * jnp.sin(angle))[None, :, :, None]
    four = jnp.stack(
        [four[0] * twist_cos - four[1] * twist_sin, four[0] * twist_sin + four[1] * twist_cos]
    )
    four = jnp.einsum("sacqb,sqtd->tadcb", four, dft_matrix(rows_q, sign), precision=highest)
    return four.reshape(2, outer, length, inner)


def rows_then_turn(block):
    return jnp.swapaxes(transform(block, -1.0), 2, 3)


def forward_along(block):
    return transform(block, -1.0)


def turn_then_rows(block):
    return transform(jnp.swapaxes(block, 2, 3), 1.0)


def local(noise, spectrum, assay, measure_weights, measure_owner, measure_cell, measure_pencils):
    size_x, size_y, depth = noise.shape
    half = spectrum.shape[0] // 2
    tables = jnp.stack(arranged_tables(depth, half, -1.0))
    spectral = jnp.einsum("xyz,sqz->sqyx", noise, tables, precision=highest)
    spectral = rows_then_turn(
        lax.all_to_all(spectral, "wide", split_axis=1, concat_axis=2, tiled=True)
    )
    spectral = forward_along(
        lax.all_to_all(spectral, "narrow", split_axis=3, concat_axis=2, tiled=True)
    )
    scaled = spectrum * (1.0 / (CELLS_FIRST * CELLS_SECOND * CELLS_THIRD))
    spectral = transform(spectral * scaled[None], 1.0)
    spectral = turn_then_rows(
        lax.all_to_all(spectral, "narrow", split_axis=2, concat_axis=3, tiled=True)
    )
    cos_rows, sin_rows = arranged_tables(depth, half, 1.0)
    inverse_tables = jnp.stack([cos_rows, -sin_rows])
    field = jnp.einsum(
        "sqyx,sqz->xyz",
        lax.all_to_all(spectral, "wide", split_axis=2, concat_axis=1, tiled=True),
        inverse_tables,
        precision=highest,
    )
    n_wide = lax.axis_size("wide")
    n_narrow = lax.axis_size("narrow")
    owner_device = measure_owner.reshape(-1)
    count = owner_device.shape[0]
    capacity = max(4, 4 * count // (n_wide * n_narrow))
    row_index = jnp.arange(count, dtype=jnp.int32)
    earlier = row_index[None, :] < row_index[:, None]
    same_owner = owner_device[None, :] == owner_device[:, None]
    slot_position = jnp.sum(same_owner & earlier, axis=1, dtype=jnp.int32)
    wide_target = owner_device // n_narrow
    narrow_target = owner_device % n_narrow
    weight_holder = jnp.zeros((n_wide, n_narrow, capacity, TARGET_PENCILS, depth), jnp.bfloat16)
    weight_holder = weight_holder.at[wide_target, narrow_target, slot_position].set(
        measure_weights[0]
    )
    assay_buf = jnp.zeros((n_wide, n_narrow, capacity), jnp.bfloat16)
    assay_buf = assay_buf.at[wide_target, narrow_target, slot_position].set(assay[0])
    row_indices = jnp.concatenate([measure_cell[0][:, None], measure_pencils[0]], axis=1)
    index_buf = jnp.zeros((n_wide, n_narrow, capacity, TARGET_PENCILS + 1), jnp.int32)
    index_buf = index_buf.at[wide_target, narrow_target, slot_position].set(row_indices)
    weight_got, assay_got, index_got = (
        lax.all_to_all(
            lax.all_to_all(weight_holder, "wide", split_axis=0, concat_axis=0, tiled=True),
            "narrow",
            split_axis=1,
            concat_axis=1,
            tiled=True,
        ),
        lax.all_to_all(
            lax.all_to_all(assay_buf, "wide", split_axis=0, concat_axis=0, tiled=True),
            "narrow",
            split_axis=1,
            concat_axis=1,
            tiled=True,
        ),
        lax.all_to_all(
            lax.all_to_all(index_buf, "wide", split_axis=0, concat_axis=0, tiled=True),
            "narrow",
            split_axis=1,
            concat_axis=1,
            tiled=True,
        ),
    )
    index_got = index_got.reshape(-1, TARGET_PENCILS + 1)
    cell_list = index_got[:, 0]
    targets = index_got[:, 1:].reshape(-1)
    value = field.reshape(-1)[cell_list]
    resid = assay_got.reshape(-1).astype(jnp.float32) - value
    contrib = resid[:, None, None] * weight_got.reshape(-1, TARGET_PENCILS, depth).astype(
        jnp.float32
    )
    correction = (
        jnp.zeros((size_x * size_y, depth), jnp.float32).at[targets].add(contrib.reshape(-1, depth))
    )
    return field + correction.reshape(size_x, size_y, depth)


def solution(mesh):
    placed = (
        P("narrow", "wide", None),
        P("wide", None, "narrow"),
        P(("wide", "narrow"), None),
        P(("wide", "narrow"), None, None, None),
        P(("wide", "narrow"), None),
        P(("wide", "narrow"), None),
        P(("wide", "narrow"), None, None),
    )
    return jax.shard_map(
        local, mesh=mesh, in_specs=placed, out_specs=P("narrow", "wide", None), check_vma=False
    )
```

profile of v0, /device:TPU:16, one launch (start us, length us, event | category | flops | bytes accessed | tf_op | source)
XLA Modules:
  0.0 602.8 jit_solution(5593420963950159069)
XLA Ops:
  1.6 6.0 %convolution_bitcast_fusion = f32[2,128,32,128]{3,1,2,0:T(8,128)S(1)} fusion(f32[128,32,128]{2,1,0:T(8,128)} %param.7, f32[1,128,128]{2,1,0:T(8,128)S(1)} %get-tuple-element.23, f32[1,128,128]{2,1,0:T(8,128)S(1)} %get-tuple-element.22), kind=kOutput, calls=%fused_computation.45 | convolution fusion | flops 1610645504 | bytes 6422528 | tf_op jit(solution)/shard_map/xyz,sqz->sqyx/dot_general | solution.py:81
  7.7 4.4 copy.272
  12.1 8.3 %all-to-all-start = ((f32[2,128,32,128]{3,2,0,1:T(8,128)}), f32[2,128,32,128]{3,2,0,1:T(8,128)}, u32[]{:S(2)}, u32[]{:S(2)}) async-start(f32[2,128,32,128]{3,2,0,1:T(8,128)} %copy.272), calls=%async_computation | async-start | bytes 8388608 | tf_op jit(solution)/shard_map/all_to_all | solution.py:83
  21.7 28.0 %scatter_fusion = s32[32,8,8,5]{3,2,1,0:T(8,128)S(1)} fusion(s32[32,8,8,5]{3,2,1,0:T(8,128)S(1)} %broadcast_in_dim.15, s32[512]{0:T(512)S(1)} %bitcast.210, s32[512,5]{1,0:T(8,128)S(1)} %copy.300), kind=kCustom, calls=%fused_computation.1 | custom fusion | bytes 36864 | tf_op jit(solution)/shard_map/scatter | solution.py:120
  52.5 29.6 %scatter_fusion.1 = bf16[32,8,8]{0,2,1:T(8,128)(2,1)S(1)} fusion(bf16[32,8,8]{0,2,1:T(8,128)(2,1)S(1)} %broadcast_in_dim.16, s32[512]{0:T(512)S(1)} %bitcast.211, bf16[512]{0:T(512)(128)(2,1)S(1)} %reduce), kind=kCustom, calls=%fused_computation.2 | custom fusion | bytes 9216 | tf_op jit(solution)/shard_map/scatter | solution.py:117
  83.7 7.3 %all-to-all-start.6 = ((bf16[32,8,8]{2,1,0:T(8,128)(2,1)}), bf16[32,8,8]{2,1,0:T(8,128)(2,1)S(1)}, u32[]{:S(2)}, u32[]{:S(2)}) async-start(bf16[32,8,8]{2,1,0:T(8,128)(2,1)} %copy.305), calls=%async_computation.6 | async-start | bytes 131072 | tf_op jit(solution)/shard_map/all_to_all | solution.py:130
  93.8 5.6 fusion.24
  102.2 7.6 %all-to-all-start.4 = ((s32[32,1,320]{2,1,0:T(1,128)}), s32[32,1,320]{2,1,0:T(1,128)S(1)}, u32[]{:S(2)}, u32[]{:S(2)}) async-start(s32[32,1,320]{2,1,0:T(1,128)} %reshape.696), calls=%async_computation.4 | async-start | bytes 98304 | tf_op jit(solution)/shard_map/all_to_all | solution.py:137
  109.8 6.6 %fusion.27 = f32[2,4,128,8,128]{4,2,3,1,0:T(8,128)S(1)} fusion(f32[2,4,8,128,128]{4,2,3,1,0:T(8,128)} %pad_maximum_fusion, f32[1,128,2,128]{1,3,0,2:T(8,128)S(1)} %get-tuple-element.14, f32[1,128,2,128]{1,3,0,2:T(8,128)S(1)} %get-tuple-element.15), kind=kOutput, calls=%fused_computation.38 | convolution fusion | flops 3221291008 | bytes 8650752 | tf_op jit(solution)/shard_map/sacqb,sqtd->tadcb/dot_general | solution.py:61
  118.8 4.7 copy.280
  123.5 8.6 %all-to-all-start.1 = ((f32[2,4,128,1024]{2,1,0,3:T(4,128)}), f32[2,4,128,1024]{2,1,0,3:T(4,128)}, u32[]{:S(2)}, u32[]{:S(2)}) async-start(f32[2,4,128,1024]{2,1,0,3:T(4,128)} %copy.280), calls=%async_computation.1 | async-start | bytes 8388608 | tf_op jit(solution)/shard_map/all_to_all | solution.py:86
  135.3 57.9 %scatter_fusion.2 = bf16[32,8,8,4,128]{4,3,2,1,0:T(4,128)(2,1)} fusion(bf16[32,8,8,4,128]{4,3,2,1,0:T(4,128)(2,1)} %broadcast_in_dim.17, s32[512]{0:T(512)S(1)} %bitcast.212, bf16[512,4,128]{2,1,0:T(4,128)(2,1)S(1)} %bitcast.229), kind=kCustom, calls=%fused_computation.3 | custom fusion | bytes 1579008 | tf_op jit(solution)/shard_map/scatter | solution.py:113
  198.3 30.5 %all-to-all-done.1 = f32[2,4,128,1024]{2,1,0,3:T(4,128)} async-done(((f32[2,4,128,1024]{2,1,0,3:T(4,128)}), f32[2,4,128,1024]{2,1,0,3:T(4,128)}, u32[]{:S(2)}, u32[]{:S(2)}) %all-to-all-start.1) | async-done | bytes 4194336 | tf_op jit(solution)/shard_map/all_to_all | solution.py:86
  232.2 4.2 copy.336
  236.4 7.8 %fusion.45 = f32[2,4,8,128,128]{4,2,3,1,0:T(8,128)} fusion(f32[2,4,128,8,128]{4,3,0,2,1:T(8,128)} %copy.336, f32[1,8,2,8]{1,3,0,2:T(8,128)S(1)} %copy.270, f32[1,8,2,8]{1,3,0,2:T(8,128)S(1)} %copy.269), kind=kOutput, calls=%fused_computation.44 | convolution fusion | flops 201326848 | bytes 8389632 | tf_op jit(solution)/shard_map/sapqb,sptc->tacqb/dot_general | solution.py:50
  244.2 7.1 %all-to-all-start.5 = ((s32[8,1,1280]{2,1,0:T(1,128)}), s32[8,1,1280]{2,1,0:T(1,128)S(1)}, u32[]{:S(2)}, u32[]{:S(2)}) async-start(s32[8,1,1280]{2,1,0:T(1,128)} %reshape.698), calls=%async_computation.5 | async-start | bytes 81920 | tf_op jit(solution)/shard_map/all_to_all | solution.py:136
  251.4 4.8 multiply_subtract_fusion.2
  259.5 7.8 %all-to-all-start.8 = ((bf16[32,8,8,4,128]{4,3,2,1,0:T(4,128)(2,1)}), bf16[32,8,8,4,128]{4,3,2,1,0:T(4,128)(2,1)}, u32[]{:S(2)}, u32[]{:S(2)}) async-start(bf16[32,8,8,4,128]{4,3,2,1,0:T(4,128)(2,1)} %scatter_fusion.2), calls=%async_computation.8 | async-start | bytes 4194304 | tf_op jit(solution)/shard_map/all_to_all | solution.py:123
  277.2 5.8 fusion.33
  283.8 4.1 fusion.36
  290.4 4.7 copy.289
  295.1 5.0 all-to-all-start.2
  303.8 93.1 %all-to-all-done.2 = f32[2,4,1024,128]{3,1,0,2:T(4,128)} async-done(((f32[2,4,1024,128]{3,1,0,2:T(4,128)}), f32[2,4,1024,128]{3,1,0,2:T(4,128)}, u32[]{:S(2)}, u32[]{:S(2)}) %all-to-all-start.2) | async-done | bytes 4194336 | tf_op jit(solution)/shard_map/all_to_all | solution.py:91
  400.5 5.0 copy.290
  405.5 5.4 copy.292
  411.0 5.4 fusion.39
  423.8 4.7 copy.296
  428.4 21.6 %all-to-all-done.9 = bf16[32,8,8,4,128]{4,3,2,0,1:T(4,128)(2,1)S(1)} async-done(((bf16[32,8,8,4,128]{4,3,2,0,1:T(4,128)(2,1)}), bf16[32,8,8,4,128]{4,3,2,0,1:T(4,128)(2,1)S(1)}, u32[]{:S(2)}, u32[]{:S(2)}) %all-to-all-start.9) | async-done | bytes 2097184 | tf_op jit(solution)/shard_map/all_to_all | solution.py:122
  450.0 7.8 %all-to-all-start.3 = ((f32[2,4,1024,128]{3,1,0,2:T(4,128)}), f32[2,4,1024,128]{3,1,0,2:T(4,128)}, u32[]{:S(2)}, u32[]{:S(2)}) async-start(f32[2,4,1024,128]{3,1,0,2:T(4,128)} %copy.296), calls=%async_computation.3 | async-start | bytes 8388608 | tf_op jit(solution)/shard_map/all_to_all | solution.py:97
  464.7 44.2 %all-to-all-done.3 = f32[2,4,1024,128]{3,1,0,2:T(4,128)} async-done(((f32[2,4,1024,128]{3,1,0,2:T(4,128)}), f32[2,4,1024,128]{3,1,0,2:T(4,128)}, u32[]{:S(2)}, u32[]{:S(2)}) %all-to-all-start.3) | async-done | bytes 4194336 | tf_op jit(solution)/shard_map/all_to_all | solution.py:97
  520.7 11.8 %gather_fusion = f32[2048]{0:T(1024)S(1)} fusion(f32[524288]{0:T(1024)S(1)} %bitcast.213, s32[2048]{0:T(1024)S(1)} %broadcast_clamp_fusion), kind=kCustom, calls=%fused_computation | custom fusion | bytes 24576 | tf_op jit(solution)/shard_map/gather | solution.py:147
  533.5 59.9 %scatter_custom_fusion.3 = f32[4096,128]{1,0:T(8,128)} fusion(s32[8192]{0:T(1024)S(1)} %bitcast.232, f32[8192,128]{1,0:T(8,128)} %bitcast.214, f32[8192]{0:T(1024)S(1)} %mul.834, f32[]{:T(128)} %constant.178.clone.1), kind=kCustom, calls=%fused_computation.35 | custom fusion | flops 2097152 | bytes 6324228 | tf_op jit(solution)/shard_map/scatter-add | solution.py:153
  (112 shorter events, 86.5 us)
Async XLA Ops:
  1.0 0.6 copy-start.1
  12.1 9.0 %copy-start.9 = (s32[1,512,4]{1,2,0:T(4,128)S(1)}, s32[1,512,4]{1,2,0:T(4,128)}, u32[]{:S(2)}) copy-start(s32[1,512,4]{1,2,0:T(4,128)} %param.13) | copy-start | bytes 24580
  12.1 9.0 %copy-start.11 = (s32[1,512]{1,0:T(1,128)S(1)}, s32[1,512]{1,0:T(1,128)}, u32[]{:S(2)}) copy-start(s32[1,512]{1,0:T(1,128)} %param.12) | copy-start | bytes 6148
  12.1 9.2 %copy-start.8 = (s32[1,512]{1,0:T(1,128)S(1)}, s32[1,512]{1,0:T(1,128)}, u32[]{:S(2)}) copy-start(s32[1,512]{1,0:T(1,128)} %param.11) | copy-start | bytes 6148
  12.1 71.6 %all-to-all-start = ((f32[2,128,32,128]{3,2,0,1:T(8,128)}), f32[2,128,32,128]{3,2,0,1:T(8,128)}, u32[]{:S(2)}, u32[]{:S(2)}) async-start(f32[2,128,32,128]{3,2,0,1:T(8,128)} %copy.272), calls=%async_computation | async-start | bytes 8388608 | tf_op jit(solution)/shard_map/all_to_all | solution.py:83
  21.1 78.4 %copy-start.3 = (f32[8,128]{0,1:T(8,128)}, f32[8,128]{0,1:T(8,128)S(1)}, u32[]{:S(2)}) copy-start(f32[8,128]{0,1:T(8,128)S(1)} %copy.277) | copy-start | bytes 12292
  21.1 31.3 %copy-start.10 = (bf16[1,512]{1,0:T(2,128)(2,1)S(1)}, bf16[1,512]{1,0:T(2,128)(2,1)}, u32[]{:S(2)}) copy-start(bf16[1,512]{1,0:T(2,128)(2,1)} %param.9) | copy-start | bytes 3076
  83.7 18.6 %all-to-all-start.6 = ((bf16[32,8,8]{2,1,0:T(8,128)(2,1)}), bf16[32,8,8]{2,1,0:T(8,128)(2,1)S(1)}, u32[]{:S(2)}, u32[]{:S(2)}) async-start(bf16[32,8,8]{2,1,0:T(8,128)(2,1)} %copy.305), calls=%async_computation.6 | async-start | bytes 131072 | tf_op jit(solution)/shard_map/all_to_all | solution.py:130
  102.2 21.2 %all-to-all-start.4 = ((s32[32,1,320]{2,1,0:T(1,128)}), s32[32,1,320]{2,1,0:T(1,128)S(1)}, u32[]{:S(2)}, u32[]{:S(2)}) async-start(s32[32,1,320]{2,1,0:T(1,128)} %reshape.696), calls=%async_computation.4 | async-start | bytes 98304 | tf_op jit(solution)/shard_map/all_to_all | solution.py:137
  123.5 11.8 %copy-start.6 = (bf16[1,512,4,128]{3,2,1,0:T(4,128)(2,1)S(1)}, bf16[1,512,4,128]{3,2,1,0:T(4,128)(2,1)}, u32[]{:S(2)}) copy-start(bf16[1,512,4,128]{3,2,1,0:T(4,128)(2,1)} %param.10) | copy-start | bytes 1572868
  123.5 105.4 %all-to-all-start.1 = ((f32[2,4,128,1024]{2,1,0,3:T(4,128)}), f32[2,4,128,1024]{2,1,0,3:T(4,128)}, u32[]{:S(2)}, u32[]{:S(2)}) async-start(f32[2,4,128,1024]{2,1,0,3:T(4,128)} %copy.280), calls=%async_computation.1 | async-start | bytes 8388608 | tf_op jit(solution)/shard_map/all_to_all | solution.py:86
  228.8 15.4 %all-to-all-start.7 = ((bf16[8,2,128]{2,1,0:T(2,128)(2,1)}), bf16[8,2,128]{2,1,0:T(2,128)(2,1)S(1)}, u32[]{:S(2)}, u32[]{:S(2)}) async-start(bf16[8,2,128]{2,1,0:T(2,128)(2,1)} %reshape.694), calls=%async_computation.7 | async-start | bytes 8192 | tf_op jit(solution)/shard_map/all_to_all | solution.py:129
  236.4 15.0 %copy-start.4 = (f32[8,128]{0,1:T(8,128)S(1)}, f32[8,128]{0,1:T(8,128)}, u32[]{:S(2)}) copy-start(f32[8,128]{0,1:T(8,128)} %copy-done.3) | copy-start | bytes 12292
  244.2 15.2 %all-to-all-start.5 = ((s32[8,1,1280]{2,1,0:T(1,128)}), s32[8,1,1280]{2,1,0:T(1,128)S(1)}, u32[]{:S(2)}, u32[]{:S(2)}) async-start(s32[8,1,1280]{2,1,0:T(1,128)} %reshape.698), calls=%async_computation.5 | async-start | bytes 81920 | tf_op jit(solution)/shard_map/all_to_all | solution.py:136
  259.5 35.6 %all-to-all-start.8 = ((bf16[32,8,8,4,128]{4,3,2,1,0:T(4,128)(2,1)}), bf16[32,8,8,4,128]{4,3,2,1,0:T(4,128)(2,1)}, u32[]{:S(2)}, u32[]{:S(2)}) async-start(bf16[32,8,8,4,128]{4,3,2,1,0:T(4,128)(2,1)} %scatter_fusion.2), calls=%async_computation.8 | async-start | bytes 4194304 | tf_op jit(solution)/shard_map/all_to_all | solution.py:123
  277.2 5.8 copy-start.5
  295.1 101.8 %all-to-all-start.2 = ((f32[2,4,1024,128]{3,1,0,2:T(4,128)}), f32[2,4,1024,128]{3,1,0,2:T(4,128)}, u32[]{:S(2)}, u32[]{:S(2)}) async-start(f32[2,4,1024,128]{3,1,0,2:T(4,128)} %copy.289), calls=%async_computation.2 | async-start | bytes 8388608 | tf_op jit(solution)/shard_map/all_to_all | solution.py:91
  396.9 53.1 %all-to-all-start.9 = ((bf16[32,8,8,4,128]{4,3,2,0,1:T(4,128)(2,1)}), bf16[32,8,8,4,128]{4,3,2,0,1:T(4,128)(2,1)S(1)}, u32[]{:S(2)}, u32[]{:S(2)}) async-start(bf16[32,8,8,4,128]{4,3,2,0,1:T(4,128)(2,1)} %copy.309), calls=%async_computation.9 | async-start | bytes 4194304 | tf_op jit(solution)/shard_map/all_to_all | solution.py:122
  450.0 58.9 %all-to-all-start.3 = ((f32[2,4,1024,128]{3,1,0,2:T(4,128)}), f32[2,4,1024,128]{3,1,0,2:T(4,128)}, u32[]{:S(2)}, u32[]{:S(2)}) async-start(f32[2,4,1024,128]{3,1,0,2:T(4,128)} %copy.296), calls=%async_computation.3 | async-start | bytes 8388608 | tf_op jit(solution)/shard_map/all_to_all | solution.py:97
  511.9 2.7 copy-start.2
  512.0 2.7 copy-start.7
  533.5 62.9 %copy-start = (f32[128,32,128]{0,2,1:T(8,128)S(1)}, f32[128,32,128]{0,2,1:T(8,128)}, u32[]{:S(2)}) copy-start(f32[128,32,128]{0,2,1:T(8,128)} %convolution_bitcast_fusion.1) | copy-start | bytes 6291460
where the time goes:
time: 610 us; the launch traced here: 603 us
  local copies, waits for them, and re-layouts  207 us (34%)
  waiting for transfers between devices  193 us (32%)
  other arithmetic  82 us (13%)
  starting transfers between devices  66.5 us (11%)
  matrix products  53.3 us (9%)
    all_to_all x1, waiting for transfers between devices, local(): lax.all_to_all(spectral, 'narrow', split_axis=2, concat_axis=3, tiled=True)  93.1 us
    scatter-add x1, other arithmetic, local(): jnp.zeros((size_x * size_y, depth), jnp.float32).at[targets]  59.9 us
    scatter x1, local copies, waits for them, and re-layouts, local(): weight_holder.at[wide_target, narrow_target, slot_position]  57.9 us
    all_to_all x1, waiting for transfers between devices, local(): lax.all_to_all(spectral, 'wide', split_axis=2, concat_axis=1, tiled=True)  44.2 us
    all_to_all x1, waiting for transfers between devices, local(): lax.all_to_all(spectral, 'narrow', split_axis=3, concat_axis=2, tiled=True)  30.5 us
    scatter x2, local copies, waits for them, and re-layouts, local(): assay_buf.at[wide_target, narrow_target, slot_position].set(assay[0])  30.3 us
    scatter x2, local copies, waits for them, and re-layouts, local(): index_buf.at[wide_target, narrow_target, slot_position].set(row_indices)  29.7 us
    dot_general x4, matrix products, transform(): jnp.einsum('sapqb,sptc->tacqb', four, dft_matrix(rows_p, sign), precision...  24.6 us
  transfers between devices with their start and end apart: 10, of which 5 were waited for; matrix products, arithmetic and copies ran while one was open for 39% of the time, Pallas kernels for 0%

commit v1 on v0

--- a/solution.py
+++ b/solution.py
@@ -9,6 +9,22 @@
 CELLS_THIRD = 128
 TARGET_PENCILS = 4
 highest = lax.Precision.HIGHEST
+
+
+def pairwise_exchange(value, axis, split, join):
+    ways, here = (lax.axis_size(axis), lax.axis_index(axis))
+    width = value.shape[split] // ways
+    shape = list(value.shape)
+    shape[split] = width
+    height = shape[join]
+    shape[join] = height * ways
+    full = jnp.zeros(shape, value.dtype)
+    for mask in range(ways):
+        part = lax.dynamic_slice_in_dim(value, (here ^ mask) * width, width, axis=split)
+        if mask:
+            part = lax.ppermute(part, axis, [(d, d ^ mask) for d in range(ways)])
+        full = lax.dynamic_update_slice_in_dim(full, part, (here ^ mask) * height, axis=join)
+    return full
 
 
 def pair_tables(cosine, sine):
@@ -119,12 +135,11 @@
     index_buf = jnp.zeros((n_wide, n_narrow, capacity, TARGET_PENCILS + 1), jnp.int32)
     index_buf = index_buf.at[wide_target, narrow_target, slot_position].set(row_indices)
     weight_got, assay_got, index_got = (
-        lax.all_to_all(
+        pairwise_exchange(
             lax.all_to_all(weight_holder, "wide", split_axis=0, concat_axis=0, tiled=True),
             "narrow",
-            split_axis=1,
-            concat_axis=1,
-            tiled=True,
+            1,
+            1,
         ),
         lax.all_to_all(
             lax.all_to_all(assay_buf, "wide", split_axis=0, concat_axis=0, tiled=True),

time: 610 us -> 589 us (0.966)
  waiting for transfers between devices: 193 us -> 163 us
  starting transfers between devices: 66.5 us -> 74.8 us
    all_to_all x1, waiting for transfers between devices: 30.5 us -> 90.9 us  [local(): lax.all_to_all(spectral, 'narrow', split_axis=3, concat_axis=2, tiled=True)]
    all_to_all x1, waiting for transfers between devices: 93.1 us -> 33.5 us  [local(): lax.all_to_all(spectral, 'narrow', split_axis=2, concat_axis=3, tiled=True)]
    all_to_all x1, waiting for transfers between devices: 44.2 us -> 0.01 us  [local(): lax.all_to_all(spectral, 'wide', split_axis=2, concat_axis=1, tiled=True)]
    ppermute x0 -> x7, waiting for transfers between devices: none -> 38.5 us  [pairwise_exchange(): part = lax.ppermute(part, axis, [(d, d ^ mask) for d in range(ways)])]
    all_to_all x1 -> x0, waiting for transfers between devices: 21.6 us -> none  [local(): lax.all_to_all(lax.all_to_all(weight_holder, 'wide', split_axis=0, concat...]
    ppermute x0 -> x7, starting transfers between devices: none -> 10.2 us  [pairwise_exchange(): part = lax.ppermute(part, axis, [(d, d ^ mask) for d in range(ways)])]
  transfers between devices with their start and end apart: 10 -> 16, of which waited for: 5 -> 8; matrix products, arithmetic and copies ran while one was open for 39% -> 41% of each run, Pallas kernels for 0% -> 0%
where the time goes in v1:
time: 589 us; the launch traced here: 581 us
  local copies, waits for them, and re-layouts  213 us (36%)
  waiting for transfers between devices  163 us (28%)
  other arithmetic  76.2 us (13%)
  starting transfers between devices  74.8 us (13%)
  matrix products  53.7 us (9%)
    all_to_all x1, waiting for transfers between devices, local(): lax.all_to_all(spectral, 'narrow', split_axis=3, concat_axis=2, tiled=True)  90.9 us
    scatter x1, local copies, waits for them, and re-layouts, local(): weight_holder.at[wide_target, narrow_target, slot_position]  60.1 us
    scatter-add x1, other arithmetic, local(): jnp.zeros((size_x * size_y, depth), jnp.float32).at[targets]  59.5 us
    ppermute x7, waiting for transfers between devices, pairwise_exchange(): part = lax.ppermute(part, axis, [(d, d ^ mask) for d in range(ways)])  38.5 us
    all_to_all x1, waiting for transfers between devices, local(): lax.all_to_all(spectral, 'narrow', split_axis=2, concat_axis=3, tiled=True)  33.5 us
    scatter x2, local copies, waits for them, and re-layouts, local(): assay_buf.at[wide_target, narrow_target, slot_position].set(assay[0])  30.3 us
    scatter x2, local copies, waits for them, and re-layouts, local(): index_buf.at[wide_target, narrow_target, slot_position].set(row_indices)  29.7 us
    dot_general x4, matrix products, transform(): jnp.einsum('sapqb,sptc->tacqb', four, dft_matrix(rows_p, sign), precision...  22.6 us
  transfers between devices with their start and end apart: 16, of which 8 were waited for; matrix products, arithmetic and copies ran while one was open for 41% of the time, Pallas kernels for 0%

profile of v1, /device:TPU:16, one launch (start us, length us, event | category | flops | bytes accessed | tf_op | source)
XLA Modules:
  0.0 581.3 jit_solution(13469354830271019915)
XLA Ops:
  1.6 6.0 %convolution_bitcast_fusion = f32[2,128,32,128]{3,1,2,0:T(8,128)S(1)} fusion(f32[128,32,128]{2,1,0:T(8,128)} %param.7, f32[1,128,128]{2,1,0:T(8,128)S(1)} %get-tuple-element.31, f32[1,128,128]{2,1,0:T(8,128)S(1)} %get-tuple-element.30), kind=kOutput, calls=%fused_computation.45 | convolution fusion | flops 1610645504 | bytes 6422528 | tf_op jit(solution)/shard_map/xyz,sqz->sqyx/dot_general | solution.py:97
  7.6 4.5 copy.218
  12.1 8.0 %all-to-all-start = ((f32[2,128,32,128]{3,2,0,1:T(8,128)}), f32[2,128,32,128]{3,2,0,1:T(8,128)}, u32[]{:S(2)}, u32[]{:S(2)}) async-start(f32[2,128,32,128]{3,2,0,1:T(8,128)} %copy.218), calls=%async_computation | async-start | bytes 8388608 | tf_op jit(solution)/shard_map/all_to_all | solution.py:99
  21.4 28.0 %scatter_fusion = s32[32,8,8,5]{3,2,1,0:T(8,128)S(1)} fusion(s32[32,8,8,5]{3,2,1,0:T(8,128)S(1)} %broadcast_in_dim.13, s32[512]{0:T(512)S(1)} %bitcast.211, s32[512,5]{1,0:T(8,128)S(1)} %copy.246), kind=kCustom, calls=%fused_computation.1 | custom fusion | bytes 36864 | tf_op jit(solution)/shard_map/scatter | solution.py:136
  52.1 29.6 %scatter_fusion.1 = bf16[32,8,8]{0,2,1:T(8,128)(2,1)S(1)} fusion(bf16[32,8,8]{0,2,1:T(8,128)(2,1)S(1)} %broadcast_in_dim.14, s32[512]{0:T(512)S(1)} %bitcast.212, bf16[512]{0:T(512)(128)(2,1)S(1)} %reduce), kind=kCustom, calls=%fused_computation.2 | custom fusion | bytes 9216 | tf_op jit(solution)/shard_map/scatter | solution.py:133
  83.3 7.3 %all-to-all-start.6 = ((bf16[32,8,8]{2,1,0:T(8,128)(2,1)}), bf16[32,8,8]{2,1,0:T(8,128)(2,1)S(1)}, u32[]{:S(2)}, u32[]{:S(2)}) async-start(bf16[32,8,8]{2,1,0:T(8,128)(2,1)} %copy.251), calls=%async_computation.6 | async-start | bytes 131072 | tf_op jit(solution)/shard_map/all_to_all | solution.py:145
  93.5 5.6 fusion.23
  101.9 7.8 %all-to-all-start.4 = ((s32[32,1,320]{2,1,0:T(1,128)}), s32[32,1,320]{2,1,0:T(1,128)S(1)}, u32[]{:S(2)}, u32[]{:S(2)}) async-start(s32[32,1,320]{2,1,0:T(1,128)} %reshape.696), calls=%async_computation.4 | async-start | bytes 98304 | tf_op jit(solution)/shard_map/all_to_all | solution.py:152
  109.7 6.6 %fusion.26 = f32[2,4,128,8,128]{4,2,3,1,0:T(8,128)S(1)} fusion(f32[2,4,8,128,128]{4,2,3,1,0:T(8,128)} %pad_maximum_fusion, f32[1,128,2,128]{1,3,0,2:T(8,128)S(1)} %get-tuple-element.22, f32[1,128,2,128]{1,3,0,2:T(8,128)S(1)} %get-tuple-element.23), kind=kOutput, calls=%fused_computation.38 | convolution fusion | flops 3221291008 | bytes 8650752 | tf_op jit(solution)/shard_map/sacqb,sqtd->tadcb/dot_general | solution.py:77
  118.7 4.7 copy.226
  123.4 8.5 %all-to-all-start.1 = ((f32[2,4,128,1024]{2,1,0,3:T(4,128)}), f32[2,4,128,1024]{2,1,0,3:T(4,128)}, u32[]{:S(2)}, u32[]{:S(2)}) async-start(f32[2,4,128,1024]{2,1,0,3:T(4,128)} %copy.226), calls=%async_computation.1 | async-start | bytes 8388608 | tf_op jit(solution)/shard_map/all_to_all | solution.py:102
  137.8 90.9 %all-to-all-done.1 = f32[2,4,128,1024]{2,1,0,3:T(4,128)} async-done(((f32[2,4,128,1024]{2,1,0,3:T(4,128)}), f32[2,4,128,1024]{2,1,0,3:T(4,128)}, u32[]{:S(2)}, u32[]{:S(2)}) %all-to-all-start.1) | async-done | bytes 4194336 | tf_op jit(solution)/shard_map/all_to_all | solution.py:102
  236.1 5.6 fusion.44
  249.9 6.0 %fusion.32 = f32[2,4,8,128,128]{4,2,3,1,0:T(8,128)S(1)} fusion(f32[2,4,8,128,128]{4,3,2,1,0:T(8,128)S(1)} %bitcast_multiply_fusion, f32[1,8,2,8]{1,3,0,2:T(8,128)S(1)} %copy.213, f32[1,8,2,8]{1,3,0,2:T(8,128)S(1)} %copy.212), kind=kOutput, calls=%fused_computation.40 | convolution fusion | flops 201326848 | bytes 8389632 | tf_op jit(solution)/shard_map/sapqb,sptc->tacqb/dot_general | solution.py:66
  258.8 7.1 %all-to-all-start.5 = ((s32[8,1,1280]{2,1,0:T(1,128)}), s32[8,1,1280]{2,1,0:T(1,128)S(1)}, u32[]{:S(2)}, u32[]{:S(2)}) async-start(s32[8,1,1280]{2,1,0:T(1,128)} %reshape.698), calls=%async_computation.5 | async-start | bytes 81920 | tf_op jit(solution)/shard_map/all_to_all | solution.py:151
  265.9 6.6 %fusion.35 = f32[2,4,128,8,128]{4,2,3,1,0:T(8,128)S(1)} fusion(f32[2,4,8,128,128]{4,2,3,1,0:T(8,128)} %pad_maximum_fusion.2, f32[1,128,2,128]{1,3,2,0:T(8,128)S(1)} %get-tuple-element.24, f32[1,128,2,128]{1,3,2,0:T(8,128)S(1)} %get-tuple-element.21), kind=kOutput, calls=%fused_computation.41 | convolution fusion | flops 3221291008 | bytes 8650752 | tf_op jit(solution)/shard_map/sacqb,sqtd->tadcb/dot_general | solution.py:77
  274.8 4.7 copy.235
  279.6 7.4 %all-to-all-start.2 = ((f32[2,4,1024,128]{3,1,0,2:T(4,128)}), f32[2,4,1024,128]{3,1,0,2:T(4,128)}, u32[]{:S(2)}, u32[]{:S(2)}) async-start(f32[2,4,1024,128]{3,1,0,2:T(4,128)} %copy.235), calls=%async_computation.2 | async-start | bytes 8388608 | tf_op jit(solution)/shard_map/all_to_all | solution.py:107
  289.3 60.1 %scatter_fusion.2 = bf16[32,8,8,4,128]{4,3,2,1,0:T(4,128)(2,1)} fusion(bf16[32,8,8,4,128]{4,3,2,1,0:T(4,128)(2,1)} %broadcast.896.clone, s32[512]{0:T(512)S(1)} %bitcast.213, bf16[512,4,128]{2,1,0:T(4,128)(2,1)S(1)} %bitcast.229), kind=kCustom, calls=%fused_computation.3 | custom fusion | bytes 1579008 | tf_op jit(solution)/shard_map/scatter | solution.py:129
  349.4 33.5 %all-to-all-done.2 = f32[2,4,1024,128]{3,1,0,2:T(4,128)} async-done(((f32[2,4,1024,128]{3,1,0,2:T(4,128)}), f32[2,4,1024,128]{3,1,0,2:T(4,128)}, u32[]{:S(2)}, u32[]{:S(2)}) %all-to-all-start.2) | async-done | bytes 4194336 | tf_op jit(solution)/shard_map/all_to_all | solution.py:107
  382.8 7.4 %all-to-all-start.8 = ((bf16[32,8,8,4,128]{4,3,2,1,0:T(4,128)(2,1)}), bf16[32,8,8,4,128]{4,3,2,1,0:T(4,128)(2,1)S(1)}, u32[]{:S(2)}, u32[]{:S(2)}) async-start(bf16[32,8,8,4,128]{4,3,2,1,0:T(4,128)(2,1)} %scatter_fusion.2), calls=%async_computation.8 | async-start | bytes 4194304 | tf_op jit(solution)/shard_map/all_to_all | solution.py:139
  390.2 5.0 copy.236
  395.2 5.4 copy.238
  400.7 5.4 fusion.38
  413.5 4.7 copy.242
  418.2 7.8 %all-to-all-start.3 = ((f32[2,4,1024,128]{3,1,0,2:T(4,128)}), f32[2,4,1024,128]{3,1,0,2:T(4,128)}, u32[]{:S(2)}, u32[]{:S(2)}) async-start(f32[2,4,1024,128]{3,1,0,2:T(4,128)} %copy.242), calls=%async_computation.3 | async-start | bytes 8388608 | tf_op jit(solution)/shard_map/all_to_all | solution.py:113
  441.3 5.1 collective-permute-done
  447.2 15.6 %collective-permute-done.1 = bf16[32,1,8,4,128]{4,3,2,1,0:T(4,128)(2,1)S(1)} collective-permute-done((bf16[32,1,8,4,128]{4,3,2,1,0:T(4,128)(2,1)S(1)}, bf16[32,1,8,4,128]{4,3,2,1,0:T(4,128)(2,1)S(1)}, u32[]{:S(2)}, u32[]{:S(2)}) %collective-permute-start.1) | collective-permute-done | bytes 262176 | tf_op jit(solution)/shard_map/ppermute | solution.py:25
  465.5 7.4 %collective-permute-done.2 = bf16[32,1,8,4,128]{4,3,2,1,0:T(4,128)(2,1)S(1)} collective-permute-done((bf16[32,1,8,4,128]{4,3,2,1,0:T(4,128)(2,1)S(1)}, bf16[32,1,8,4,128]{4,3,2,1,0:T(4,128)(2,1)S(1)}, u32[]{:S(2)}, u32[]{:S(2)}) %collective-permute-start.2) | collective-permute-done | bytes 262176 | tf_op jit(solution)/shard_map/ppermute | solution.py:25
  473.8 4.5 collective-permute-done.3
  499.3 11.8 %gather_fusion = f32[2048]{0:T(1024)S(1)} fusion(f32[524288]{0:T(1024)S(1)} %bitcast.214, s32[2048]{0:T(1024)S(1)} %broadcast_clamp_fusion), kind=kCustom, calls=%fused_computation | custom fusion | bytes 24576 | tf_op jit(solution)/shard_map/gather | solution.py:162
  512.1 59.5 %scatter_custom_fusion.3 = f32[4096,128]{1,0:T(8,128)} fusion(s32[8192]{0:T(1024)S(1)} %bitcast.232, bf16[8192,128]{1,0:T(8,128)(2,1)} %bitcast.109, f32[8192]{0:T(1024)S(1)} %mul.834, f32[]{:T(128)} %constant.186.clone.1), kind=kCustom, calls=%fused_computation.10 | custom fusion | flops 3145728 | bytes 4227076 | tf_op jit(solution)/shard_map/scatter-add | solution.py:168
  (129 shorter events, 102.1 us)
Async XLA Ops:
  1.0 0.6 copy-start.1
  12.1 8.7 %copy-start.9 = (s32[1,512,4]{1,2,0:T(4,128)S(1)}, s32[1,512,4]{1,2,0:T(4,128)}, u32[]{:S(2)}) copy-start(s32[1,512,4]{1,2,0:T(4,128)} %param.13) | copy-start | bytes 24580
  12.1 8.7 %copy-start.11 = (s32[1,512]{1,0:T(1,128)S(1)}, s32[1,512]{1,0:T(1,128)}, u32[]{:S(2)}) copy-start(s32[1,512]{1,0:T(1,128)} %param.12) | copy-start | bytes 6148
  12.1 8.9 %copy-start.8 = (s32[1,512]{1,0:T(1,128)S(1)}, s32[1,512]{1,0:T(1,128)}, u32[]{:S(2)}) copy-start(s32[1,512]{1,0:T(1,128)} %param.11) | copy-start | bytes 6148
  12.1 71.2 %all-to-all-start = ((f32[2,128,32,128]{3,2,0,1:T(8,128)}), f32[2,128,32,128]{3,2,0,1:T(8,128)}, u32[]{:S(2)}, u32[]{:S(2)}) async-start(f32[2,128,32,128]{3,2,0,1:T(8,128)} %copy.218), calls=%async_computation | async-start | bytes 8388608 | tf_op jit(solution)/shard_map/all_to_all | solution.py:99
  20.8 78.3 %copy-start.3 = (f32[8,128]{0,1:T(8,128)}, f32[8,128]{0,1:T(8,128)S(1)}, u32[]{:S(2)}) copy-start(f32[8,128]{0,1:T(8,128)S(1)} %copy.223) | copy-start | bytes 12292
  49.3 2.8 copy-start.10
  83.3 18.6 %all-to-all-start.6 = ((bf16[32,8,8]{2,1,0:T(8,128)(2,1)}), bf16[32,8,8]{2,1,0:T(8,128)(2,1)S(1)}, u32[]{:S(2)}, u32[]{:S(2)}) async-start(bf16[32,8,8]{2,1,0:T(8,128)(2,1)} %copy.251), calls=%async_computation.6 | async-start | bytes 131072 | tf_op jit(solution)/shard_map/all_to_all | solution.py:145
  101.9 21.5 %all-to-all-start.4 = ((s32[32,1,320]{2,1,0:T(1,128)}), s32[32,1,320]{2,1,0:T(1,128)S(1)}, u32[]{:S(2)}, u32[]{:S(2)}) async-start(s32[32,1,320]{2,1,0:T(1,128)} %reshape.696), calls=%async_computation.4 | async-start | bytes 98304 | tf_op jit(solution)/shard_map/all_to_all | solution.py:152
  123.4 105.3 %all-to-all-start.1 = ((f32[2,4,128,1024]{2,1,0,3:T(4,128)}), f32[2,4,128,1024]{2,1,0,3:T(4,128)}, u32[]{:S(2)}, u32[]{:S(2)}) async-start(f32[2,4,128,1024]{2,1,0,3:T(4,128)} %copy.226), calls=%async_computation.1 | async-start | bytes 8388608 | tf_op jit(solution)/shard_map/all_to_all | solution.py:102
  228.7 30.1 %all-to-all-start.7 = ((bf16[8,2,128]{2,1,0:T(2,128)(2,1)}), bf16[8,2,128]{2,1,0:T(2,128)(2,1)S(1)}, u32[]{:S(2)}, u32[]{:S(2)}) async-start(bf16[8,2,128]{2,1,0:T(2,128)(2,1)} %reshape.694), calls=%async_computation.7 | async-start | bytes 8192 | tf_op jit(solution)/shard_map/all_to_all | solution.py:144
  236.1 5.6 copy-start.4
  249.9 6.0 %copy-start.5 = (f32[8,128]{0,1:T(8,128)S(1)}, f32[8,128]{0,1:T(8,128)}, u32[]{:S(2)}) copy-start(f32[8,128]{0,1:T(8,128)} %copy.231) | copy-start | bytes 12292
  258.8 20.8 %all-to-all-start.5 = ((s32[8,1,1280]{2,1,0:T(1,128)}), s32[8,1,1280]{2,1,0:T(1,128)S(1)}, u32[]{:S(2)}, u32[]{:S(2)}) async-start(s32[8,1,1280]{2,1,0:T(1,128)} %reshape.698), calls=%async_computation.5 | async-start | bytes 81920 | tf_op jit(solution)/shard_map/all_to_all | solution.py:151
  279.6 103.3 %all-to-all-start.2 = ((f32[2,4,1024,128]{3,1,0,2:T(4,128)}), f32[2,4,1024,128]{3,1,0,2:T(4,128)}, u32[]{:S(2)}, u32[]{:S(2)}) async-start(f32[2,4,1024,128]{3,1,0,2:T(4,128)} %copy.235), calls=%async_computation.2 | async-start | bytes 8388608 | tf_op jit(solution)/shard_map/all_to_all | solution.py:107
  287.0 2.3 copy-start.6
  382.8 35.4 %all-to-all-start.8 = ((bf16[32,8,8,4,128]{4,3,2,1,0:T(4,128)(2,1)}), bf16[32,8,8,4,128]{4,3,2,1,0:T(4,128)(2,1)S(1)}, u32[]{:S(2)}, u32[]{:S(2)}) async-start(bf16[32,8,8,4,128]{4,3,2,1,0:T(4,128)(2,1)} %scatter_fusion.2), calls=%async_computation.8 | async-start | bytes 4194304 | tf_op jit(solution)/shard_map/all_to_all | solution.py:139
  418.2 69.3 %all-to-all-start.3 = ((f32[2,4,1024,128]{3,1,0,2:T(4,128)}), f32[2,4,1024,128]{3,1,0,2:T(4,128)}, u32[]{:S(2)}, u32[]{:S(2)}) async-start(f32[2,4,1024,128]{3,1,0,2:T(4,128)} %copy.242), calls=%async_computation.3 | async-start | bytes 8388608 | tf_op jit(solution)/shard_map/all_to_all | solution.py:113
  433.0 13.4 %collective-permute-start = (bf16[32,1,8,4,128]{4,3,2,1,0:T(4,128)(2,1)S(1)}, bf16[32,1,8,4,128]{4,3,2,1,0:T(4,128)(2,1)S(1)}, u32[]{:S(2)}, u32[]{:S(2)}) collective-permute-start(bf16[32,1,8,4,128]{4,3,2,1,0:T(4,128)(2,1)S(1)} %get-tuple-element.19), channel_id=1, source_target_pairs={{0,1},{1,0},{2,3},{3,2},{4,5},{5,4},{6,7},{7,6},{8,9},{9,8},{10,11... | collective-permute-start | bytes 786440 | tf_op jit(solution)/shard_map/ppermute | solution.py:25
  433.3 29.5 %collective-permute-start.1 = (bf16[32,1,8,4,128]{4,3,2,1,0:T(4,128)(2,1)S(1)}, bf16[32,1,8,4,128]{4,3,2,1,0:T(4,128)(2,1)S(1)}, u32[]{:S(2)}, u32[]{:S(2)}) collective-permute-start(bf16[32,1,8,4,128]{4,3,2,1,0:T(4,128)(2,1)S(1)} %get-tuple-element.18), channel_id=1, source_target_pairs={{0,2},{1,3},{2,0},{3,1},{4,6},{5,7},{6,4},{7,5},{8,10},{9,11},{10,... | collective-permute-start | bytes 786440 | tf_op jit(solution)/shard_map/ppermute | solution.py:25
  433.4 39.6 %collective-permute-start.2 = (bf16[32,1,8,4,128]{4,3,2,1,0:T(4,128)(2,1)S(1)}, bf16[32,1,8,4,128]{4,3,2,1,0:T(4,128)(2,1)S(1)}, u32[]{:S(2)}, u32[]{:S(2)}) collective-permute-start(bf16[32,1,8,4,128]{4,3,2,1,0:T(4,128)(2,1)S(1)} %get-tuple-element.17), channel_id=1, source_target_pairs={{0,3},{1,2},{2,1},{3,0},{4,7},{5,6},{6,5},{7,4},{8,11},{9,10},{10,... | collective-permute-start | bytes 786440 | tf_op jit(solution)/shard_map/ppermute | solution.py:25
  437.5 40.7 %collective-permute-start.3 = (bf16[32,1,8,4,128]{4,3,2,1,0:T(4,128)(2,1)S(1)}, bf16[32,1,8,4,128]{4,3,2,1,0:T(4,128)(2,1)S(1)}, u32[]{:S(2)}, u32[]{:S(2)}) collective-permute-start(bf16[32,1,8,4,128]{4,3,2,1,0:T(4,128)(2,1)S(1)} %get-tuple-element.16), channel_id=1, source_target_pairs={{0,4},{1,5},{2,6},{3,7},{4,0},{5,1},{6,2},{7,3},{8,12},{9,13},{10,... | collective-permute-start | bytes 786440 | tf_op jit(solution)/shard_map/ppermute | solution.py:25
  437.8 44.1 %collective-permute-start.4 = (bf16[32,1,8,4,128]{4,3,2,1,0:T(4,128)(2,1)S(1)}, bf16[32,1,8,4,128]{4,3,2,1,0:T(4,128)(2,1)S(1)}, u32[]{:S(2)}, u32[]{:S(2)}) collective-permute-start(bf16[32,1,8,4,128]{4,3,2,1,0:T(4,128)(2,1)S(1)} %get-tuple-element.15), channel_id=1, source_target_pairs={{0,5},{1,4},{2,7},{3,6},{4,1},{5,0},{6,3},{7,2},{8,13},{9,12},{10,... | collective-permute-start | bytes 786440 | tf_op jit(solution)/shard_map/ppermute | solution.py:25
  446.4 36.3 %collective-permute-start.5 = (bf16[32,1,8,4,128]{4,3,2,1,0:T(4,128)(2,1)S(1)}, bf16[32,1,8,4,128]{4,3,2,1,0:T(4,128)(2,1)S(1)}, u32[]{:S(2)}, u32[]{:S(2)}) collective-permute-start(bf16[32,1,8,4,128]{4,3,2,1,0:T(4,128)(2,1)S(1)} %get-tuple-element.14), channel_id=1, source_target_pairs={{0,6},{1,7},{2,4},{3,5},{4,2},{5,3},{6,0},{7,1},{8,14},{9,15},{10,... | collective-permute-start | bytes 786440 | tf_op jit(solution)/shard_map/ppermute | solution.py:25
  462.8 23.9 %collective-permute-start.6 = (bf16[32,1,8,4,128]{4,3,2,1,0:T(4,128)(2,1)S(1)}, bf16[32,1,8,4,128]{4,3,2,1,0:T(4,128)(2,1)S(1)}, u32[]{:S(2)}, u32[]{:S(2)}) collective-permute-start(bf16[32,1,8,4,128]{4,3,2,1,0:T(4,128)(2,1)S(1)} %get-tuple-element.13), channel_id=1, source_target_pairs={{0,7},{1,6},{2,5},{3,4},{4,3},{5,2},{6,1},{7,0},{8,15},{9,14},{10,... | collective-permute-start | bytes 786440 | tf_op jit(solution)/shard_map/ppermute | solution.py:25
  490.5 2.7 copy-start.2
  490.6 2.7 copy-start.7
  571.5 3.1 copy-start
